TPU v7x, 32 devices: a whole 2x2x4 slice. The times are simulated.
32 devices in a mesh: pipe: 2 (over y), lat: 4 (over x, core), lon: 4 (over z).
Axes of the slice: x: 2, y: 2, z: 4, core: 2. Of those that a mesh axis runs over, the one named last changes fastest.
Arguments:
- field: bfloat16 [192, 64, 1024], P(None, 'lat', 'lon'), may hold values from -6 to 6
- conv_weight: bfloat16 [192, 1728], replicated, may hold values from -0.15625 to 0.15625
- conv_bias: float32 [192], replicated, may hold values from -3 to 3
- expand_weight: bfloat16 [768, 192], replicated, may hold values from -0.4375 to 0.4375
- expand_bias: float32 [768], replicated, may hold values from -3 to 3
- project_weight: bfloat16 [192, 768], replicated, may hold values from -0.21875 to 0.21875
- project_bias: float32 [192], replicated, may hold values from -3 to 3
- out_cotangent: bfloat16 [192, 32, 512], P(None, 'lat', 'lon'), may hold values from -6 to 6
- dropout_key: int32 [2], replicated, may hold values from 0 to 1073741823
Outputs:
- section_fields: bfloat16 [2, 192, 32, 512], P('pipe', None, 'lat', 'lon')
- conv_grad: float32 [192, 1728], replicated
- conv_bias_grad: float32 [192], replicated
- expand_grad: float32 [768, 192], replicated
- expand_bias_grad: float32 [768], replicated
- project_grad: float32 [192, 768], replicated
- project_bias_grad: float32 [192], replicated
All inputs are finite; a program needn't handle non-finite values.
Results may differ from a plain program's by a relative error of at most 0.0056.
Values may be sent and summed in bfloat16 or wider, within the bound.
A program may use at most 64 MiB of HBM per device.

v0:
```python
import jax
import jax.numpy as jnp
from jax import lax
from jax.sharding import PartitionSpec as P

MIXER_ONE = -2048144789
MIXER_TWO = -1028477387
GOLDEN_STEP = -1640531535
KEEP_LEVEL = 819
KEEP_SCALE = 1024.0 / 819.0


def passed_along(value, axis, steps):
    count = lax.axis_size(axis)
    pairs = [(source, (source + steps) % count) for source in range(count)]
    return lax.ppermute(value, axis, pairs)


def shifted_2(block, axis, distance):
    devices = range(lax.axis_size(axis))
    route = [(i - distance, i) for i in devices if i - distance in devices]
    return lax.ppermute(block, axis, route)


def shifted(number, places):
    return lax.shift_right_logical(number, jnp.full_like(number, places))


def scramble(number):
    number = number ^ shifted(number, 16)
    number = number * jnp.int32(MIXER_ONE)
    number = number ^ shifted(number, 13)
    number = number * jnp.int32(MIXER_TWO)
    return number ^ shifted(number, 16)


def keep_mask(cell_index, dropout_key):
    salt = scramble(dropout_key[0] + scramble(dropout_key[1]))
    hashed = scramble(cell_index * jnp.int32(GOLDEN_STEP) + salt)
    bucket = jnp.bitwise_and(shifted(hashed, 8), jnp.int32(1023))
    return jnp.where(bucket < KEEP_LEVEL, jnp.float32(KEEP_SCALE), jnp.float32(0.0))


def gelu_slope(point, incoming):
    return jax.vjp(jax.nn.gelu, point)[1](incoming)[0]


def outer_sum(left, right):
    return lax.dot_general(
        left, right, (((1,), (1,)), ((), ())), preferred_element_type=jnp.float32
    )


def contract_first(weight, right):
    return lax.dot_general(
        weight, right, (((0,), (0,)), ((), ())), preferred_element_type=jnp.float32
    )


def parity_planes(padded, out_rows, out_cols):
    channels = padded.shape[0]
    even_sized = jnp.pad(padded, ((0, 0), (0, 1), (0, 1)))
    split = even_sized.reshape(channels, out_rows + 1, 2, out_cols + 1, 2)
    return jnp.transpose(split, (2, 4, 0, 1, 3))


def tap_slice(planes, tap_row, tap_col, out_rows, out_cols):
    plane = planes[tap_row % 2, tap_col % 2]
    channels = plane.shape[0]
    row_from = tap_row // 2
    col_from = tap_col // 2
    piece = lax.slice(
        plane, (0, row_from, col_from), (channels, row_from + out_rows, col_from + out_cols)
    )
    return piece.reshape(channels, out_rows * out_cols)


def convolve(conv_weight, planes, out_rows, out_cols):
    channels = planes.shape[2]
    total = None
    for tap_row in range(3):
        for tap_col in range(3):
            tap = 3 * tap_row + tap_col
            term = jnp.dot(
                conv_weight[:, tap * channels : (tap + 1) * channels],
                tap_slice(planes, tap_row, tap_col, out_rows, out_cols),
                preferred_element_type=jnp.float32,
            )
            total = term if total is None else total + term
    return total


def kernel_gradient(d_half, planes, out_rows, out_cols):
    blocks = []
    for tap_row in range(3):
        for tap_col in range(3):
            blocks.append(
                outer_sum(d_half, tap_slice(planes, tap_row, tap_col, out_rows, out_cols))
            )
    return jnp.concatenate(blocks, axis=1)


def hand_over(payload):
    return passed_along(payload, "pipe", 1)


def per_device(
    field,
    conv_weight,
    conv_bias,
    expand_weight,
    expand_bias,
    project_weight,
    project_bias,
    out_cotangent,
    dropout_key,
):
    channels, row_count, col_count = field.shape
    hidden_count = expand_weight.shape[0]
    half_rows = row_count // 2
    half_cols = col_count // 2
    lat_count = lax.axis_size("lat")
    lon_count = lax.axis_size("lon")
    scale = float(half_rows * lat_count * half_cols * lon_count) ** (-0.5)
    pipe_index = lax.axis_index("pipe")
    is_encoder = pipe_index == 0
    from_above = shifted_2(field[:, row_count - 1 :, :], "lat", 1)
    mirrored = passed_along(field[:, :1, :], "lon", lon_count // 2)
    top_row = jnp.where(lax.axis_index("lat") == 0, mirrored, from_above)
    extended = jnp.concatenate([top_row, field], axis=1)
    west_edge = passed_along(extended[:, :, col_count - 1 :], "lon", 1)
    padded = jnp.concatenate([west_edge, extended], axis=2)
    row_start = 0
    cell_count = half_rows * half_cols
    planes = parity_planes(padded, half_rows, half_cols)
    row_ids = lax.axis_index("lat") * half_rows + row_start + jnp.arange(half_rows, dtype=jnp.int32)
    col_ids = lax.axis_index("lon") * half_cols + jnp.arange(half_cols, dtype=jnp.int32)
    cell_ids = (row_ids[:, None] * (half_cols * lon_count) + col_ids[None, :]).reshape(-1)
    keep = keep_mask(cell_ids, dropout_key)[None, :]

    def encode():
        pre = convolve(conv_weight, planes, half_rows, half_cols) + conv_bias[:, None]
        encoded = (jax.nn.gelu(pre) * keep).astype(jnp.bfloat16)
        return (encoded, pre)

    def encode_empty():
        return (
            jnp.zeros((channels, cell_count), jnp.bfloat16),
            jnp.zeros((channels, cell_count), jnp.float32),
        )

    def process(received):
        inner = (
            jnp.dot(expand_weight, received, preferred_element_type=jnp.float32)
            + expand_bias[:, None]
        )
        activated = jax.nn.gelu(inner).astype(jnp.bfloat16)
        processed = (
            received.astype(jnp.float32)
            + jnp.dot(project_weight, activated, preferred_element_type=jnp.float32)
            + project_bias[:, None]
        ).astype(jnp.bfloat16)
        scaled = out_cotangent.reshape(channels, cell_count).astype(jnp.float32) * scale
        cot_half = scaled.astype(jnp.bfloat16)
        project_grad = outer_sum(cot_half, activated)
        d_inner = gelu_slope(inner, contract_first(project_weight, cot_half))
        d_inner_half = d_inner.astype(jnp.bfloat16)
        expand_grad = outer_sum(d_inner_half, received)
        d_encoded = (scaled + contract_first(expand_weight, d_inner_half)).astype(jnp.bfloat16)
        flat = jnp.concatenate(
            [
                expand_grad.reshape(-1),
                jnp.sum(d_inner, axis=1),
                project_grad.reshape(-1),
                jnp.sum(scaled, axis=1),
            ]
        )
        return (processed, d_encoded, flat)

    enc_len = conv_weight.size + channels
    proc_len = 2 * expand_weight.size + hidden_count + channels

    def process_empty():
        return (
            jnp.zeros((channels, cell_count), jnp.bfloat16),
            jnp.zeros((channels, cell_count), jnp.bfloat16),
            jnp.zeros((proc_len,), jnp.float32),
        )

    def backward(pre_now, d_encoded_now):
        d_pre = gelu_slope(pre_now, d_encoded_now.astype(jnp.float32) * keep)
        conv_grad = kernel_gradient(d_pre.astype(jnp.bfloat16), planes, half_rows, half_cols)
        return jnp.concatenate([conv_grad.reshape(-1), jnp.sum(d_pre, axis=1)])

    def backward_empty():
        return jnp.zeros((enc_len,), jnp.float32)

    encoded, pre_saved = lax.cond(is_encoder, encode, encode_empty)
    received = hand_over(encoded)
    processed, d_encoded, flat_proc = lax.cond(is_encoder, process_empty, lambda: process(received))
    returned = hand_over(d_encoded)
    flat_enc = lax.cond(is_encoder, lambda: backward(pre_saved, returned), backward_empty)
    section_fields = jnp.where(is_encoder, encoded, processed).reshape(
        1, channels, half_rows, half_cols
    )
    combined = jnp.concatenate([flat_enc, flat_proc])
    total = lax.psum(combined, ("pipe", "lat", "lon"))
    enc_total = total[:enc_len]
    proc_total = total[enc_len:]
    weight_count = conv_weight.size
    conv_grad = enc_total[:weight_count].reshape(conv_weight.shape)
    conv_bias_grad = enc_total[weight_count:]
    expand_count = expand_weight.size
    expand_grad = proc_total[:expand_count].reshape(expand_weight.shape)
    expand_bias_grad = proc_total[expand_count : expand_count + hidden_count]
    project_start = expand_count + hidden_count
    project_grad = proc_total[project_start : project_start + expand_count].reshape(
        project_weight.shape
    )
    project_bias_grad = proc_total[project_start + expand_count :]
    return (
        section_fields,
        conv_grad,
        conv_bias_grad,
        expand_grad,
        expand_bias_grad,
        project_grad,
        project_bias_grad,
    )


def solution(mesh):
    placed = (P(None, "lat", "lon"), P(), P(), P(), P(), P(), P(), P(None, "lat", "lon"), P())
    return jax.shard_map(
        per_device,
        mesh=mesh,
        in_specs=placed,
        out_specs=(P("pipe", None, "lat", "lon"), P(), P(), P(), P(), P(), P()),
        check_vma=False,
    )
```

profile of v0, /device:TPU:0, one launch (start us, length us, event | category | flops | bytes accessed | tf_op | source)
XLA Modules:
  0.0 278.3 jit_solution(14114148621795843833)
XLA Ops:
  7.2 1.7 fusion.114
  8.9 4.1 %collective-permute-start = (bf16[192,1,256]{2,0,1:T(8,128)(2,1)S(1)}, bf16[192,1,256]{2,0,1:T(8,128)(2,1)S(1)}, u32[]{:S(2)}, u32[]{:S(2)}) collective-permute-start(bf16[192,1,256]{2,0,1:T(8,128)(2,1)S(1)} %copy.47), channel_id=1, source_target_pairs={{0,2},{1,3},{2,0},{3,1},{4,6},{5,7},{6,4},{7,5},{8,10},{9,11},{10,... | collective-permute-start | bytes 294920 | tf_op jit(solution)/shard_map/ppermute | solution.py:16
  13.0 1.5 collective-permute-start.1
  14.5 1.3 fusion.115
  17.9 3.6 %copy.37 = bf16[192,16,256]{0,1,2:T(8,128)(2,1)S(1)} copy(bf16[192,16,256]{2,1,0:T(8,128)(2,1)} %param.15) | data formatting | bytes 3145728 | tf_op args[0]
  21.8 1.6 collective-permute-start.2
  23.4 3.9 %collective-permute-done.2 = bf16[192,17,1]{0,1,2:T(8,128)(2,1)S(1)} collective-permute-done((bf16[192,17,1]{0,1,2:T(8,128)(2,1)S(1)}, bf16[192,17,1]{0,1,2:T(8,128)(2,1)S(1)}, u32[]{:S(2)}, u32[]{:S(2)}) %collective-permute-start.2) | collective-permute-done | bytes 6560 | tf_op jit(solution)/shard_map/ppermute | solution.py:16
  27.3 2.7 fusion.97
  30.0 6.4 %reshape.189 = bf16[192,9,2,129,2]{0,2,1,4,3:T(2,128)(2,1)} reshape(bf16[192,18,258]{0,1,2:T(8,128)(2,1)} %fusion.97) | data formatting | bytes 3566592 | tf_op jit(solution)/shard_map/reshape | solution.py:63
  36.4 3.5 %copy.150 = bf16[192,9,2,129,2]{0,4,3,2,1:T(2,128)(2,1)S(1)} copy(bf16[192,9,2,129,2]{0,2,1,4,3:T(2,128)(2,1)} %reshape.189) | data formatting | bytes 3566592 | tf_op jit(solution)/shard_map/reshape | solution.py:63
  40.0 19.9 %conditional.3 = ((bf16[192,1024]{1,0:T(8,128)(2,1)}, f32[192,1024]{1,0:T(8,128)S(1)})) conditional(s32[]{:T(128)} %convert_element_type.39, () %tuple.30, (bf16[192,1728]{1,0:T(8,128)(2,1)}, bf16[2,2,192,9,129]{2,1,4,0,3:T(2,128)(2,1)S(1)}, f32[192]{0:T(256)S(1)}, f32[1,1024]{1,0:T(1,128)S(1)}) %tuple.92), branch_computations={%region_0.1_spmd, %region_1.2_spmd} | conditional | flops 683212800 | bytes 35056676 | solution.py:198
  40.0 11.7 %copy.39 = bf16[2,2,192,9,129]{4,3,2,1,0:T(8,128)(2,1)} copy(bf16[2,2,192,9,129]{2,1,4,0,3:T(2,128)(2,1)S(1)} %get-tuple-element.104) | data formatting | bytes 3566592 | tf_op jit(solution)/shard_map
  51.7 3.2 %slice_bitcast_fusion = (bf16[192,9,129]{2,1,0:T(8,128)(2,1)S(1)}, bf16[192,9,129]{2,1,0:T(8,128)(2,1)S(1)}, bf16[192,9,129]{2,1,0:T(8,128)(2,1)S(1)}, bf16[192,9,129]{2,1,0:T(8,128)(2,1)S(1)}) fusion(bf16[2,2,192,9,129]{4,3,2,1,0:T(8,128)(2,1)} %copy.39), kind=kLoop, calls=%fused_computation | loop fusion | bytes 3566592 | tf_op jit(solution)/shard_map/cond/branch_1_fun/squeeze | solution.py:68
  58.6 1.2 fusion.9
  59.9 12.1 %collective-permute-done.3 = bf16[192,1024]{1,0:T(8,128)(2,1)S(1)} collective-permute-done((bf16[192,1024]{1,0:T(8,128)(2,1)}, bf16[192,1024]{1,0:T(8,128)(2,1)S(1)}, u32[]{:S(2)}, u32[]{:S(2)}) %collective-permute-start.3) | collective-permute-done | bytes 393248 | tf_op jit(solution)/shard_map/ppermute | solution.py:16
  72.4 19.1 %collective-permute-start.4 = (bf16[192,1024]{1,0:T(8,128)(2,1)S(1)}, bf16[192,1024]{1,0:T(8,128)(2,1)}, u32[]{:S(2)}, u32[]{:S(2)}) collective-permute-start(bf16[192,1024]{1,0:T(8,128)(2,1)S(1)} %get-tuple-element.59), channel_id=1, source_target_pairs={{0,16},{16,0},{1,17},{17,1},{2,18},{18,2},{3,19},{19,3},{4,20},{20... | collective-permute-start | bytes 1179656 | tf_op jit(solution)/shard_map/ppermute | solution.py:16
  91.5 9.5 %collective-permute-done.4 = bf16[192,1024]{1,0:T(8,128)(2,1)} collective-permute-done((bf16[192,1024]{1,0:T(8,128)(2,1)S(1)}, bf16[192,1024]{1,0:T(8,128)(2,1)}, u32[]{:S(2)}, u32[]{:S(2)}) %collective-permute-start.4) | collective-permute-done | bytes 393248 | tf_op jit(solution)/shard_map/ppermute | solution.py:16
  101.1 25.0 %conditional.5 = (f32[331968]{0:T(1024)S(1)}) conditional(s32[]{:T(128)} %convert_element_type.39, () %tuple.34, (bf16[192,1024]{1,0:T(8,128)(2,1)}, f32[1,1024]{1,0:T(1,128)S(1)}, f32[192,1024]{1,0:T(8,128)}, bf16[2,2,192,9,129]{2,1,4,0,3:T(2,128)(2,1)S(1)}) %tuple.88), branch_computations={%region_6.7_spmd, %region_7.9_spmd} | conditional | flops 684331008 | bytes 36876584 | solution.py:202
  101.1 11.7 %copy.41 = bf16[2,2,192,9,129]{4,3,2,1,0:T(8,128)(2,1)} copy(bf16[2,2,192,9,129]{2,1,4,0,3:T(2,128)(2,1)S(1)} %get-tuple-element.116) | data formatting | bytes 3566592 | tf_op jit(solution)/shard_map
  112.7 3.2 %slice_bitcast_fusion.4 = (bf16[192,9,129]{2,1,0:T(8,128)(2,1)S(1)}, bf16[192,9,129]{2,1,0:T(8,128)(2,1)S(1)}, bf16[192,9,129]{2,1,0:T(8,128)(2,1)S(1)}, bf16[192,9,129]{2,1,0:T(8,128)(2,1)S(1)}) fusion(bf16[2,2,192,9,129]{4,3,2,1,0:T(8,128)(2,1)} %copy.41), kind=kLoop, calls=%fused_computation.80 | loop fusion | bytes 3566592 | tf_op jit(solution)/shard_map/cond/branch_1_fun/squeeze | solution.py:68
  117.1 1.6 fusion.103
  120.7 1.0 fusion.72
  121.6 1.0 fusion.78
  123.6 1.4 concatenate.13
  126.0 3.2 %pad_maximum_fusion.2 = f32[627840]{0:T(1024)} fusion(f32[295872]{0:T(1024)} %copy-done.4, f32[331968]{0:T(1024)S(1)} %get-tuple-element.183), kind=kLoop, calls=%fused_computation.131 | loop fusion | flops 627840 | bytes 5022720 | tf_op jit(solution)/shard_map/concatenate | solution.py:206
  131.2 129.0 %all-reduce.3.cloned.1.call-done = f32[627840]{0:T(1024)} async-done(((f32[627840]{0:T(1024)}), f32[627840]{0:T(1024)}) %all-reduce.3.cloned.1.call-update) | async-done | bytes 2511376 | tf_op jit(solution)/shard_map/psum | solution.py:207
  260.2 1.3 slice-done
  261.5 1.5 reshape.186
  263.0 2.6 fusion.113
  265.7 1.4 reshape.187
  267.1 1.1 copy.42
  268.1 2.0 reshape.188
  (71 shorter events, 12.7 us)
Async XLA Ops:
  7.2 253.0 %all-reduce.3.cloned.1.call-start = ((), (), s32[]{:S(2)}) async-start(), calls=%async_computation | async-start | bytes 5029888 | tf_op jit(solution)/shard_map/psum | solution.py:207
  8.9 12.6 %collective-permute-start = (bf16[192,1,256]{2,0,1:T(8,128)(2,1)S(1)}, bf16[192,1,256]{2,0,1:T(8,128)(2,1)S(1)}, u32[]{:S(2)}, u32[]{:S(2)}) collective-permute-start(bf16[192,1,256]{2,0,1:T(8,128)(2,1)S(1)} %copy.47), channel_id=1, source_target_pairs={{0,2},{1,3},{2,0},{3,1},{4,6},{5,7},{6,4},{7,5},{8,10},{9,11},{10,... | collective-permute-start | bytes 294920 | tf_op jit(solution)/shard_map/ppermute | solution.py:16
  13.0 8.5 %collective-permute-start.1 = (bf16[192,1,256]{2,0,1:T(8,128)(2,1)S(1)}, bf16[192,1,256]{2,0,1:T(8,128)(2,1)S(1)}, u32[]{:S(2)}, u32[]{:S(2)}) collective-permute-start(bf16[192,1,256]{2,0,1:T(8,128)(2,1)S(1)} %copy.48), channel_id=1, source_target_pairs={{0,4},{4,8},{8,12},{1,5},{5,9},{9,13},{2,6},{6,10},{10,14},{3,7},{... | collective-permute-start | bytes 294920 | tf_op jit(solution)/shard_map/ppermute | solution.py:22
  21.8 5.5 %collective-permute-start.2 = (bf16[192,17,1]{0,1,2:T(8,128)(2,1)S(1)}, bf16[192,17,1]{0,1,2:T(8,128)(2,1)S(1)}, u32[]{:S(2)}, u32[]{:S(2)}) collective-permute-start(bf16[192,17,1]{0,1,2:T(8,128)(2,1)S(1)} %pad_maximum_fusion.3), channel_id=1, source_target_pairs={{0,1},{1,2},{2,3},{3,0},{4,5},{5,6},{6,7},{7,4},{8,9},{9,10},{10,1... | collective-permute-start | bytes 19592 | tf_op jit(solution)/shard_map/ppermute | solution.py:16
  36.4 3.5 %copy-start.19 = (f32[192]{0:T(256)S(1)}, f32[192]{0:T(256)}, u32[]{:S(2)}) copy-start(f32[192]{0:T(256)} %param.17) | copy-start | bytes 2308
  40.0 32.0 %copy-start.14 = (bf16[768,192]{0,1:T(8,128)(2,1)S(1)}, bf16[768,192]{0,1:T(8,128)(2,1)}, u32[]{:S(2)}) copy-start(bf16[768,192]{0,1:T(8,128)(2,1)} %param.18) | copy-start | bytes 884740
  40.0 32.0 %copy-start.17 = (f32[192]{0:T(256)S(1)}, f32[192]{0:T(256)}, u32[]{:S(2)}) copy-start(f32[192]{0:T(256)} %param.21) | copy-start | bytes 2308
  40.0 32.0 %copy-start.18 = (f32[768]{0:T(1024)S(1)}, f32[768]{0:T(1024)}, u32[]{:S(2)}) copy-start(f32[768]{0:T(1024)} %param.19) | copy-start | bytes 9220
  55.0 1.1 copy-start.12
  59.9 12.1 %copy-start.5 = (f32[192,1024]{1,0:T(8,128)}, f32[192,1024]{1,0:T(8,128)S(1)}, u32[]{:S(2)}) copy-start(f32[192,1024]{1,0:T(8,128)S(1)} %get-tuple-element.60) | copy-start | bytes 2359300
  59.9 12.1 %collective-permute-start.3 = (bf16[192,1024]{1,0:T(8,128)(2,1)}, bf16[192,1024]{1,0:T(8,128)(2,1)S(1)}, u32[]{:S(2)}, u32[]{:S(2)}) collective-permute-start(bf16[192,1024]{1,0:T(8,128)(2,1)} %get-tuple-element.57), channel_id=1, source_target_pairs={{0,16},{16,0},{1,17},{17,1},{2,18},{18,2},{3,19},{19,3},{4,20},{20... | collective-permute-start | bytes 1179656 | tf_op jit(solution)/shard_map/ppermute | solution.py:16
  72.4 28.6 %copy-start.4 = (f32[295872]{0:T(1024)}, f32[295872]{0:T(1024)S(1)}, u32[]{:S(2)}) copy-start(f32[295872]{0:T(1024)S(1)} %get-tuple-element.61) | copy-start | bytes 3550468
  72.4 28.6 %copy-start.7 = (bf16[192,1024]{1,0:T(8,128)(2,1)}, bf16[192,1024]{1,0:T(8,128)(2,1)S(1)}, u32[]{:S(2)}) copy-start(bf16[192,1024]{1,0:T(8,128)(2,1)S(1)} %get-tuple-element.58) | copy-start | bytes 1179652
  72.4 28.6 %collective-permute-start.4 = (bf16[192,1024]{1,0:T(8,128)(2,1)S(1)}, bf16[192,1024]{1,0:T(8,128)(2,1)}, u32[]{:S(2)}, u32[]{:S(2)}) collective-permute-start(bf16[192,1024]{1,0:T(8,128)(2,1)S(1)} %get-tuple-element.59), channel_id=1, source_target_pairs={{0,16},{16,0},{1,17},{17,1},{2,18},{18,2},{3,19},{19,3},{4,20},{20... | collective-permute-start | bytes 1179656 | tf_op jit(solution)/shard_map/ppermute | solution.py:16
  116.0 1.1 copy-start.6
  129.2 1.0 copy-start.8
  129.2 1.1 copy-start.9
  260.2 1.3 slice-start
  265.7 4.5 %copy-start.3 = (f32[627840]{0:T(1024)S(1)}, f32[627840]{0:T(1024)}, u32[]{:S(2)}) copy-start(f32[627840]{0:T(1024)} %all-reduce.3.cloned.1.call-done) | copy-start | bytes 7534084
Sparse Core Ops, SparseCore 0:
  129.4 130.8 all-reduce.2
where the time goes:
time: 279 us; the launch traced here: 278 us
  waiting for transfers between devices  155 us (56%)
  local copies, waits for them, and re-layouts  64.8 us (23%)
  starting transfers between devices  26.4 us (9%)
  between operations  16.2 us (6%)
  matrix products  8.09 us (3%)
  other arithmetic  7.87 us (3%)
    psum x1, waiting for transfers between devices, per_device(): total = lax.psum(combined, ('pipe', 'lat', 'lon'))  129 us
    ppermute x4, waiting for transfers between devices, passed_along(): return lax.ppermute(value, axis, pairs)  25.5 us
    ppermute x4, starting transfers between devices, passed_along(): return lax.ppermute(value, axis, pairs)  24.9 us
    another operation x5, local copies, waits for them, and re-layouts  23.6 us
    reshape x2, local copies, waits for them, and re-layouts, parity_planes(): split = even_sized.reshape(channels, out_rows + 1, 2, out_cols + 1, 2)  9.93 us
    unnamed x25, local copies, waits for them, and re-layouts  6.66 us
    squeeze x2, local copies, waits for them, and re-layouts, tap_slice(): plane = planes[tap_row % 2, tap_col % 2]  6.47 us
  transfers between devices with their start and end apart: 6, of which 4 were waited for; matrix products, arithmetic and copies ran while one was open for 2% of the time, Pallas kernels for 0%

commit v1 on v0

--- a/solution.py
+++ b/solution.py
@@ -204,7 +204,7 @@
         1, channels, half_rows, half_cols
     )
     combined = jnp.concatenate([flat_enc, flat_proc])
-    total = lax.psum(combined, ("pipe", "lat", "lon"))
+    total = lax.psum(lax.psum(combined, ("lat", "lon")), "pipe")
     enc_total = total[:enc_len]
     proc_total = total[enc_len:]
     weight_count = conv_weight.size

time: 279 us -> 318 us (1.14)
  waiting for transfers between devices: 155 us -> 194 us
    psum x1 -> x2, waiting for transfers between devices: 129 us -> 169 us  [per_device(): total = lax.psum(lax.psum(combined, ('lat', 'lon')), 'pipe')]
  transfers between devices with their start and end apart: 6 -> 7, of which waited for: 4 -> 5; matrix products, arithmetic and copies ran while one was open for 2% -> 2% of each run, Pallas kernels for 0% -> 0%
where the time goes in v1:
time: 318 us; the launch traced here: 317 us
  waiting for transfers between devices  194 us (61%)
  local copies, waits for them, and re-layouts  63.7 us (20%)
  starting transfers between devices  26.4 us (8%)
  between operations  16.2 us (5%)
  matrix products  8.09 us (3%)
  other arithmetic  7.82 us (2%)
    psum x2, waiting for transfers between devices, per_device(): total = lax.psum(lax.psum(combined, ('lat', 'lon')), 'pipe')  169 us
    ppermute x4, waiting for transfers between devices, passed_along(): return lax.ppermute(value, axis, pairs)  25.5 us
    ppermute x4, starting transfers between devices, passed_along(): return lax.ppermute(value, axis, pairs)  24.9 us
    another operation x5, local copies, waits for them, and re-layouts  23.6 us
    reshape x2, local copies, waits for them, and re-layouts, parity_planes(): split = even_sized.reshape(channels, out_rows + 1, 2, out_cols + 1, 2)  9.93 us
    squeeze x2, local copies, waits for them, and re-layouts, tap_slice(): plane = planes[tap_row % 2, tap_col % 2]  6.47 us
  transfers between devices with their start and end apart: 7, of which 5 were waited for; matrix products, arithmetic and copies ran while one was open for 2% of the time, Pallas kernels for 0%

profile of v1, /device:TPU:0, one launch (start us, length us, event | category | flops | bytes accessed | tf_op | source)
XLA Modules:
  0.0 317.1 jit_solution(7849952106211091627)
XLA Ops:
  7.2 1.7 fusion.114
  8.9 4.1 %collective-permute-start = (bf16[192,1,256]{2,0,1:T(8,128)(2,1)S(1)}, bf16[192,1,256]{2,0,1:T(8,128)(2,1)S(1)}, u32[]{:S(2)}, u32[]{:S(2)}) collective-permute-start(bf16[192,1,256]{2,0,1:T(8,128)(2,1)S(1)} %copy.47), channel_id=1, source_target_pairs={{0,2},{1,3},{2,0},{3,1},{4,6},{5,7},{6,4},{7,5},{8,10},{9,11},{10,... | collective-permute-start | bytes 294920 | tf_op jit(solution)/shard_map/ppermute | solution.py:16
  13.0 1.5 collective-permute-start.1
  14.5 1.3 fusion.115
  17.9 3.6 %copy.37 = bf16[192,16,256]{0,1,2:T(8,128)(2,1)S(1)} copy(bf16[192,16,256]{2,1,0:T(8,128)(2,1)} %param.15) | data formatting | bytes 3145728 | tf_op args[0]
  21.8 1.6 collective-permute-start.2
  23.4 3.9 %collective-permute-done.2 = bf16[192,17,1]{0,1,2:T(8,128)(2,1)S(1)} collective-permute-done((bf16[192,17,1]{0,1,2:T(8,128)(2,1)S(1)}, bf16[192,17,1]{0,1,2:T(8,128)(2,1)S(1)}, u32[]{:S(2)}, u32[]{:S(2)}) %collective-permute-start.2) | collective-permute-done | bytes 6560 | tf_op jit(solution)/shard_map/ppermute | solution.py:16
  27.3 2.7 fusion.97
  30.0 6.4 %reshape.189 = bf16[192,9,2,129,2]{0,2,1,4,3:T(2,128)(2,1)} reshape(bf16[192,18,258]{0,1,2:T(8,128)(2,1)} %fusion.97) | data formatting | bytes 3566592 | tf_op jit(solution)/shard_map/reshape | solution.py:63
  36.4 3.5 %copy.150 = bf16[192,9,2,129,2]{0,4,3,2,1:T(2,128)(2,1)S(1)} copy(bf16[192,9,2,129,2]{0,2,1,4,3:T(2,128)(2,1)} %reshape.189) | data formatting | bytes 3566592 | tf_op jit(solution)/shard_map/reshape | solution.py:63
  40.0 19.9 %conditional.3 = ((bf16[192,1024]{1,0:T(8,128)(2,1)}, f32[192,1024]{1,0:T(8,128)S(1)})) conditional(s32[]{:T(128)} %convert_element_type.39, () %tuple.30, (bf16[192,1728]{1,0:T(8,128)(2,1)}, bf16[2,2,192,9,129]{2,1,4,0,3:T(2,128)(2,1)S(1)}, f32[192]{0:T(256)S(1)}, f32[1,1024]{1,0:T(1,128)S(1)}) %tuple.94), branch_computations={%region_0.1_spmd, %region_1.2_spmd} | conditional | flops 683212800 | bytes 35056676 | solution.py:198
  40.0 11.7 %copy.39 = bf16[2,2,192,9,129]{4,3,2,1,0:T(8,128)(2,1)} copy(bf16[2,2,192,9,129]{2,1,4,0,3:T(2,128)(2,1)S(1)} %get-tuple-element.104) | data formatting | bytes 3566592 | tf_op jit(solution)/shard_map
  51.7 3.2 %slice_bitcast_fusion = (bf16[192,9,129]{2,1,0:T(8,128)(2,1)S(1)}, bf16[192,9,129]{2,1,0:T(8,128)(2,1)S(1)}, bf16[192,9,129]{2,1,0:T(8,128)(2,1)S(1)}, bf16[192,9,129]{2,1,0:T(8,128)(2,1)S(1)}) fusion(bf16[2,2,192,9,129]{4,3,2,1,0:T(8,128)(2,1)} %copy.39), kind=kLoop, calls=%fused_computation | loop fusion | bytes 3566592 | tf_op jit(solution)/shard_map/cond/branch_1_fun/squeeze | solution.py:68
  58.6 1.2 fusion.9
  59.9 12.1 %collective-permute-done.3 = bf16[192,1024]{1,0:T(8,128)(2,1)S(1)} collective-permute-done((bf16[192,1024]{1,0:T(8,128)(2,1)}, bf16[192,1024]{1,0:T(8,128)(2,1)S(1)}, u32[]{:S(2)}, u32[]{:S(2)}) %collective-permute-start.3) | collective-permute-done | bytes 393248 | tf_op jit(solution)/shard_map/ppermute | solution.py:16
  72.4 19.1 %collective-permute-start.4 = (bf16[192,1024]{1,0:T(8,128)(2,1)S(1)}, bf16[192,1024]{1,0:T(8,128)(2,1)}, u32[]{:S(2)}, u32[]{:S(2)}) collective-permute-start(bf16[192,1024]{1,0:T(8,128)(2,1)S(1)} %get-tuple-element.59), channel_id=1, source_target_pairs={{0,16},{16,0},{1,17},{17,1},{2,18},{18,2},{3,19},{19,3},{4,20},{20... | collective-permute-start | bytes 1179656 | tf_op jit(solution)/shard_map/ppermute | solution.py:16
  91.5 9.5 %collective-permute-done.4 = bf16[192,1024]{1,0:T(8,128)(2,1)} collective-permute-done((bf16[192,1024]{1,0:T(8,128)(2,1)S(1)}, bf16[192,1024]{1,0:T(8,128)(2,1)}, u32[]{:S(2)}, u32[]{:S(2)}) %collective-permute-start.4) | collective-permute-done | bytes 393248 | tf_op jit(solution)/shard_map/ppermute | solution.py:16
  101.1 25.0 %conditional.5 = (f32[331968]{0:T(1024)S(1)}) conditional(s32[]{:T(128)} %convert_element_type.39, () %tuple.34, (bf16[192,1024]{1,0:T(8,128)(2,1)}, f32[1,1024]{1,0:T(1,128)S(1)}, f32[192,1024]{1,0:T(8,128)}, bf16[2,2,192,9,129]{2,1,4,0,3:T(2,128)(2,1)S(1)}) %tuple.90), branch_computations={%region_6.7_spmd, %region_7.9_spmd} | conditional | flops 684331008 | bytes 36876584 | solution.py:202
  101.1 11.7 %copy.41 = bf16[2,2,192,9,129]{4,3,2,1,0:T(8,128)(2,1)} copy(bf16[2,2,192,9,129]{2,1,4,0,3:T(2,128)(2,1)S(1)} %get-tuple-element.116) | data formatting | bytes 3566592 | tf_op jit(solution)/shard_map
  112.7 3.2 %slice_bitcast_fusion.4 = (bf16[192,9,129]{2,1,0:T(8,128)(2,1)S(1)}, bf16[192,9,129]{2,1,0:T(8,128)(2,1)S(1)}, bf16[192,9,129]{2,1,0:T(8,128)(2,1)S(1)}, bf16[192,9,129]{2,1,0:T(8,128)(2,1)S(1)}) fusion(bf16[2,2,192,9,129]{4,3,2,1,0:T(8,128)(2,1)} %copy.41), kind=kLoop, calls=%fused_computation.80 | loop fusion | bytes 3566592 | tf_op jit(solution)/shard_map/cond/branch_1_fun/squeeze | solution.py:68
  117.1 1.6 fusion.103
  120.7 1.0 fusion.72
  123.6 1.4 concatenate.13
  126.0 3.1 pad_maximum_fusion.2
  129.2 96.1 %all-reduce.4.cloned.1.call-done = f32[627840]{0:T(1024)} async-done(((f32[627840]{0:T(1024)}), f32[627840]{0:T(1024)}) %all-reduce.4.cloned.1.call-update) | async-done | bytes 2511376 | tf_op jit(solution)/shard_map/psum | solution.py:207
  226.2 72.8 %all-reduce.6.cloned.1.call-done = f32[627840]{0:T(1024)} async-done(((f32[627840]{0:T(1024)}), f32[627840]{0:T(1024)}) %all-reduce.6.cloned.1.call-update) | async-done | bytes 2511376 | tf_op jit(solution)/shard_map/psum | solution.py:207
  299.1 1.3 slice-done
  300.4 1.5 reshape.186
  301.9 2.6 fusion.113
  304.5 1.4 reshape.187
  305.9 1.1 copy.42
  307.0 2.0 reshape.188
  (74 shorter events, 12.7 us)
Async XLA Ops:
  7.2 218.1 %all-reduce.4.cloned.1.call-start = ((), (), s32[]{:S(2)}) async-start(), calls=%async_computation | async-start | bytes 5029888 | tf_op jit(solution)/shard_map/psum | solution.py:207
  8.9 12.6 %collective-permute-start = (bf16[192,1,256]{2,0,1:T(8,128)(2,1)S(1)}, bf16[192,1,256]{2,0,1:T(8,128)(2,1)S(1)}, u32[]{:S(2)}, u32[]{:S(2)}) collective-permute-start(bf16[192,1,256]{2,0,1:T(8,128)(2,1)S(1)} %copy.47), channel_id=1, source_target_pairs={{0,2},{1,3},{2,0},{3,1},{4,6},{5,7},{6,4},{7,5},{8,10},{9,11},{10,... | collective-permute-start | bytes 294920 | tf_op jit(solution)/shard_map/ppermute | solution.py:16
  13.0 8.5 %collective-permute-start.1 = (bf16[192,1,256]{2,0,1:T(8,128)(2,1)S(1)}, bf16[192,1,256]{2,0,1:T(8,128)(2,1)S(1)}, u32[]{:S(2)}, u32[]{:S(2)}) collective-permute-start(bf16[192,1,256]{2,0,1:T(8,128)(2,1)S(1)} %copy.48), channel_id=1, source_target_pairs={{0,4},{4,8},{8,12},{1,5},{5,9},{9,13},{2,6},{6,10},{10,14},{3,7},{... | collective-permute-start | bytes 294920 | tf_op jit(solution)/shard_map/ppermute | solution.py:22
  21.8 5.5 %collective-permute-start.2 = (bf16[192,17,1]{0,1,2:T(8,128)(2,1)S(1)}, bf16[192,17,1]{0,1,2:T(8,128)(2,1)S(1)}, u32[]{:S(2)}, u32[]{:S(2)}) collective-permute-start(bf16[192,17,1]{0,1,2:T(8,128)(2,1)S(1)} %pad_maximum_fusion.3), channel_id=1, source_target_pairs={{0,1},{1,2},{2,3},{3,0},{4,5},{5,6},{6,7},{7,4},{8,9},{9,10},{10,1... | collective-permute-start | bytes 19592 | tf_op jit(solution)/shard_map/ppermute | solution.py:16
  36.4 3.5 %copy-start.19 = (f32[192]{0:T(256)S(1)}, f32[192]{0:T(256)}, u32[]{:S(2)}) copy-start(f32[192]{0:T(256)} %param.17) | copy-start | bytes 2308
  40.0 32.0 %copy-start.14 = (bf16[768,192]{0,1:T(8,128)(2,1)S(1)}, bf16[768,192]{0,1:T(8,128)(2,1)}, u32[]{:S(2)}) copy-start(bf16[768,192]{0,1:T(8,128)(2,1)} %param.18) | copy-start | bytes 884740
  40.0 32.0 %copy-start.17 = (f32[192]{0:T(256)S(1)}, f32[192]{0:T(256)}, u32[]{:S(2)}) copy-start(f32[192]{0:T(256)} %param.21) | copy-start | bytes 2308
  40.0 32.0 %copy-start.18 = (f32[768]{0:T(1024)S(1)}, f32[768]{0:T(1024)}, u32[]{:S(2)}) copy-start(f32[768]{0:T(1024)} %param.19) | copy-start | bytes 9220
  55.0 1.1 copy-start.12
  59.9 12.1 %copy-start.5 = (f32[192,1024]{1,0:T(8,128)}, f32[192,1024]{1,0:T(8,128)S(1)}, u32[]{:S(2)}) copy-start(f32[192,1024]{1,0:T(8,128)S(1)} %get-tuple-element.60) | copy-start | bytes 2359300
  59.9 12.1 %collective-permute-start.3 = (bf16[192,1024]{1,0:T(8,128)(2,1)}, bf16[192,1024]{1,0:T(8,128)(2,1)S(1)}, u32[]{:S(2)}, u32[]{:S(2)}) collective-permute-start(bf16[192,1024]{1,0:T(8,128)(2,1)} %get-tuple-element.57), channel_id=1, source_target_pairs={{0,16},{16,0},{1,17},{17,1},{2,18},{18,2},{3,19},{19,3},{4,20},{20... | collective-permute-start | bytes 1179656 | tf_op jit(solution)/shard_map/ppermute | solution.py:16
  72.4 28.6 %copy-start.4 = (f32[295872]{0:T(1024)}, f32[295872]{0:T(1024)S(1)}, u32[]{:S(2)}) copy-start(f32[295872]{0:T(1024)S(1)} %get-tuple-element.61) | copy-start | bytes 3550468
  72.4 28.6 %copy-start.7 = (bf16[192,1024]{1,0:T(8,128)(2,1)}, bf16[192,1024]{1,0:T(8,128)(2,1)S(1)}, u32[]{:S(2)}) copy-start(bf16[192,1024]{1,0:T(8,128)(2,1)S(1)} %get-tuple-element.58) | copy-start | bytes 1179652
  72.4 28.6 %collective-permute-start.4 = (bf16[192,1024]{1,0:T(8,128)(2,1)S(1)}, bf16[192,1024]{1,0:T(8,128)(2,1)}, u32[]{:S(2)}, u32[]{:S(2)}) collective-permute-start(bf16[192,1024]{1,0:T(8,128)(2,1)S(1)} %get-tuple-element.59), channel_id=1, source_target_pairs={{0,16},{16,0},{1,17},{17,1},{2,18},{18,2},{3,19},{19,3},{4,20},{20... | collective-permute-start | bytes 1179656 | tf_op jit(solution)/shard_map/ppermute | solution.py:16
  116.0 1.1 copy-start.6
  129.2 96.2 %copy-start.8 = (bf16[192,1024]{1,0:T(8,128)(2,1)S(1)}, bf16[192,1024]{1,0:T(8,128)(2,1)}, u32[]{:S(2)}) copy-start(bf16[192,1024]{1,0:T(8,128)(2,1)} %copy-done.7) | copy-start | bytes 1179652
  129.2 96.2 %copy-start.9 = (bf16[192,1024]{1,0:T(8,128)(2,1)S(1)}, bf16[192,1024]{1,0:T(8,128)(2,1)}, u32[]{:S(2)}) copy-start(bf16[192,1024]{1,0:T(8,128)(2,1)} %get-tuple-element.57) | copy-start | bytes 1179652
  129.2 169.9 %all-reduce.6.cloned.1.call-start = ((), (), s32[]{:S(2)}) async-start(), calls=%async_computation.1 | async-start | bytes 5029888 | tf_op jit(solution)/shard_map/psum | solution.py:207
  299.1 1.3 slice-start
  304.5 4.5 %copy-start.3 = (f32[627840]{0:T(1024)S(1)}, f32[627840]{0:T(1024)}, u32[]{:S(2)}) copy-start(f32[627840]{0:T(1024)} %all-reduce.6.cloned.1.call-done) | copy-start | bytes 7534084
Sparse Core Ops, SparseCore 0:
  129.3 95.9 all-reduce.3
  227.6 71.4 all-reduce.5
